TPU v7x, 128 devices: a whole 4x4x4 slice. The times are simulated.
128 devices in a mesh: lat: 4 (over z_hi, core), lon: 32 (over x, y, z_lo).
Axes of the slice: x: 4, y: 4, z: 4 (z_hi: 2, z_lo: 2; z = z_hi * 2 + z_lo), core: 2. Of those that a mesh axis runs over, the one named last changes fastest.
Arguments:
- tokens: bfloat16 [2, 48, 768, 512], P(None, 'lat', 'lon'), may hold values from -15 to 15
- land_mask: int32 [48, 768], P('lat', 'lon'), may hold values 0 or 1
- land_embed: float32 [512], replicated, may hold values from -3 to 3
- shifts: int32 [2, 2], replicated, may hold values from 0 to 5
- gain_attn: float32 [512], replicated, may hold values from 0.1 to 1.9
- w_qkv_fine: bfloat16 [512, 1536], replicated, may hold values from -11 to 11
- w_out_fine: bfloat16 [512, 512], replicated, may hold values from -0.75 to 0.75
- gain_mlp: float32 [512], replicated, may hold values from 0.1 to 1.9
- w_up_fine: bfloat16 [512, 2048], replicated, may hold values from -0.25 to 0.25
- w_down_fine: bfloat16 [2048, 512], replicated, may hold values from -0.125 to 0.125
- gain_merge: float32 [2048], replicated, may hold values from 0.1 to 1.9
- w_merge: bfloat16 [2048, 1024], replicated, may hold values from -0.125 to 0.125
- gain_coarse: float32 [1024], replicated, may hold values from 0.1 to 1.9
- w_qkv_coarse: bfloat16 [1024, 3072], replicated, may hold values from -11 to 11
- w_out_coarse: bfloat16 [1024, 1024], replicated, may hold values from -0.75 to 0.75
- w_expand: bfloat16 [1024, 2048], replicated, may hold values from -0.1875 to 0.1875
Outputs:
- blended: bfloat16 [2, 48, 768, 512], P(None, 'lat', 'lon')
All inputs are finite; a program needn't handle non-finite values. No bound on the sum of `land_mask` on one device may be relied on, other than what follows from the above.
Results may differ from a plain program's by a relative error of at most 0.02.
Values may be sent and summed in bfloat16 or wider, within the bound.
A program may use at most 128 MiB of HBM per device.

v0:
```python
import jax
import jax.numpy as jnp
from jax import lax
from jax.experimental import pallas as pl
from jax.experimental.pallas import tpu as pltpu
from jax.sharding import PartitionSpec as P

HEAD = 64
WLAT = 6
WLON = 12
WIN = 2 * WLAT * WLON
REACH = 5
MAIN = 128
REST = WIN - MAIN

D1 = 512
D2 = 1024
FF1 = 2048
held = MAIN + REST * (D2 // HEAD)
ROWS, COLS = 12, 24
ROWS2, COLS2 = 6, 12
TOK = 2 * ROWS * COLS
TOK2 = 2 * ROWS2 * COLS2
HALF, HALF2 = TOK // 2, TOK2 // 2
LINE = 2 * COLS
SPAN = (WLAT + REACH) * LINE

EPSILON = 1e-05
NEGATIVE = -1e30
SCALE = HEAD ** (-0.5) * 1.4426950408889634
BF = jnp.bfloat16
F32 = jnp.float32
I32 = jnp.int32
MESH = pl.DeviceIdType.MESH


def div(x, d):
    return (x * ((1 << 20) // d + 1)) >> 20


def col(n):
    return lax.broadcasted_iota(I32, (n, 1), 0)


def row(n):
    return lax.broadcasted_iota(I32, (1, n), 1)


def onehot(target, lanes):
    return jnp.where(lanes == target, 1.0, 0.0).astype(BF)


def mm(a, b):
    return lax.dot_general(a, b, (((1,), (0,)), ((), ())), preferred_element_type=F32)


def mm_nt(a, b):
    return lax.dot_general(a, b, (((1,), (1,)), ((), ())), preferred_element_type=F32)


def mm_tn(a, b):
    return lax.dot_general(a, b, (((0,), (0,)), ((), ())), preferred_element_type=F32)


def norm(x, gain):
    mean = jnp.mean(x, axis=-1, keepdims=True)
    center = x - mean
    var = jnp.mean(center * center, axis=-1, keepdims=True)
    return (center * lax.rsqrt(var + EPSILON) * gain).astype(BF)


def slot_parts(s):
    r = div(s, 24)
    rest = s - r * 24
    lev = div(rest, 12)
    return r, lev, rest - lev * 12


def own_parts(t):
    half = div(t, HALF2)
    rest = t - half * HALF2
    rl = div(rest, COLS2 // 2)
    return rl >> 1, rl & 1, half * (COLS2 // 2) + rest - rl * (COLS2 // 2)


def soften(s, bias):
    s = s + bias
    top = jnp.max(s, axis=0, keepdims=True)
    p = jnp.exp2(s * SCALE - top * SCALE)
    total = jnp.sum(p, axis=0, keepdims=True)
    return p.astype(BF), 1.0 / total


def window_attend(q_of, k_of, v_of, width, bias, put):
    heads = width // HEAD
    pairs = heads // 2
    lane = row(2 * HEAD)
    every = pl.ds(0, width)
    parts = [pl.ds(i * 2 * HEAD, 2 * HEAD) for i in range(pairs)]
    spread = REST * heads
    tiled = jnp.concatenate([q_of(pl.ds(MAIN, REST), every)] * heads, axis=0)
    own = (col(spread) >> 4) == (row(width) >> 6)
    tiled = jnp.where(own, tiled, jnp.zeros_like(tiled))
    scores = [mm_nt(k_of(every), tiled)]
    for part in parts:
        q = q_of(pl.ds(0, MAIN), part)
        zero = jnp.zeros_like(q)
        both = jnp.concatenate(
            [jnp.where(lane < HEAD, q, zero), jnp.where(lane < HEAD, zero, q)], axis=0
        )
        scores.append(mm_nt(k_of(part), both))
    weights = [soften(x, bias) for x in scores]
    results = [mm_tn(v_of(part), p) for part, (p, _) in zip([every] + parts, weights)]
    o = results[0] * weights[0][1]
    o = jnp.where((col(width) >> 6) == (row(spread) >> 4), o, 0.0)
    put(0, width, MAIN, spread, o)
    for i in range(pairs):
        o = results[i + 1] * weights[i + 1][1]
        put(i * 2 * HEAD, HEAD, 0, MAIN, o[:HEAD, :MAIN])
        put(i * 2 * HEAD + HEAD, HEAD, 0, MAIN, o[HEAD:, MAIN:])


def kernel(
    tokens, mask, embed, shifts, gain_attn, gain_mlp, gain_merge, gain_coarse,
    w_qkv_h, w_out_h, w_up_h, w_down_h, w_merge_h, w_qkv2_h, w_out2_h, w_expand_h,
    out,
    w_qkv, w_out, w_up, w_down, w_merge, w_qkv2, w_out2, w_expand,
    inputs, ext, side_out, side, sel_own, sel_side, sel_back, qkv, mixed, back_out, back_in,
    resid, acc,
    norm2, send2, ext2, sel2, sel2_own, x2, qkv2, mixed2, back2_out, last_out, back2_in,
    w_sem, send_sem, recv_sem,
):
    lat = lax.axis_index("lat")
    lon = lax.axis_index("lon")
    lat_n = lax.axis_size("lat")
    lon_n = lax.axis_size("lon")
    right = lax.rem(lon + 1, lon_n)
    left = lax.rem(lon + lon_n - 1, lon_n)
    has_up = lat > 0
    has_down = lat < lat_n - 1
    odd = lax.rem(lat, 2) == 1
    even = jnp.logical_not(odd)

    loads = []
    for i, (src, dst) in enumerate(
        [
            (w_qkv_h, w_qkv), (w_out_h, w_out), (w_up_h, w_up), (w_down_h, w_down),
            (w_merge_h, w_merge), (w_qkv2_h, w_qkv2), (w_out2_h, w_out2), (w_expand_h, w_expand),
        ]
    ):
        load = pltpu.make_async_copy(src, dst, w_sem.at[i])
        load.start()
        loads.append(load)

    barrier = pltpu.get_barrier_semaphore()

    def greet(a, b):
        pl.semaphore_signal(barrier, inc=1, device_id=(a, b), device_id_type=MESH)

    greet(lat, left)
    greet(lat, right)

    @pl.when(has_up)
    def _():
        for b in (left, lon, right):
            greet(lat - 1, b)

    @pl.when(has_down)
    def _():
        for b in (left, lon, right):
            greet(lat + 1, b)

    def remote(i, src, dst, a, b):
        return pltpu.make_async_remote_copy(
            src_ref=src, dst_ref=dst, send_sem=send_sem.at[i], recv_sem=recv_sem.at[i],
            device_id=(a, b), device_id_type=MESH,
        )

    eye = col(COLS) == row(COLS)
    add = embed[...]
    gain = gain_attn[...]
    for r in range(ROWS):
        land = jnp.sum(jnp.where(eye, mask[r : r + 1, :].astype(F32), 0.0), axis=1, keepdims=True)
        x = jnp.concatenate(
            [tokens[0, r].astype(F32) + land * add, tokens[1, r].astype(F32) + land * add], axis=0
        ).astype(BF)
        inputs[r] = x
        ext[REACH + r] = norm(x.astype(F32), gain)

    s = col(256)
    part = jnp.where(s < 128, 0, jnp.where(s < 192, 1, 2))
    within = s - jnp.where(part == 0, 0, jnp.where(part == 1, 128, 192))
    r = div(within, 10)
    rest = within - r * 10
    lev = div(rest, 5)
    c = rest - lev * 5
    r = r + jnp.where(part == 1, ROWS - REACH, 0)
    target = jnp.where(r < ROWS, r * LINE + lev * COLS + c + (COLS - REACH), -1)
    own = ext[REACH : REACH + ROWS].reshape(TOK, D1)
    side_out[...] = mm(onehot(target, row(TOK)), own).astype(BF)

    @pl.when(jnp.logical_not(has_up))
    def _():
        for at in (0, 128, 320):
            ext2[at : at + 64] = jnp.zeros((64, D2), BF)

    @pl.when(even | jnp.logical_not(has_down))
    def _():
        for at in (64, 192, 384):
            ext2[at : at + 64] = jnp.zeros((64, D2), BF)

    ext[2 * REACH + ROWS] = jnp.zeros((LINE, D1), BF)

    @pl.when(jnp.logical_not(has_up))
    def _():
        ext[0:REACH] = jnp.zeros((REACH, LINE, D1), BF)
        side[128:192] = jnp.zeros((64, D1), BF)

    @pl.when(jnp.logical_not(has_down))
    def _():
        ext[REACH + ROWS : 2 * REACH + ROWS] = jnp.zeros((REACH, LINE, D1), BF)
        side[192:256] = jnp.zeros((64, D1), BF)

    pl.semaphore_wait(
        barrier, 2 + jnp.where(has_up, 3, 0) + jnp.where(has_down, 3, 0)
    )

    go_right = remote(0, side_out.at[0:128], side.at[0:128], lat, right)
    go_down = remote(1, ext.at[ROWS : ROWS + REACH], ext.at[0:REACH], lat + 1, lon)
    go_up = remote(2, ext.at[REACH : 2 * REACH], ext.at[REACH + ROWS : 2 * REACH + ROWS], lat - 1, lon)
    go_down_right = remote(3, side_out.at[128:192], side.at[128:192], lat + 1, right)
    go_up_right = remote(4, side_out.at[192:256], side.at[192:256], lat - 1, right)

    def exchange(r_, d_, u_, dr_, ur_):
        r_.start()

        @pl.when(has_down)
        def _():
            d_.start()
            dr_.start()

        @pl.when(has_up)
        def _():
            u_.start()
            ur_.start()

    def arrived(d_, u_, dr_, ur_):
        @pl.when(has_up)
        def _():
            d_.wait_recv()
            dr_.wait_recv()

        @pl.when(has_down)
        def _():
            u_.wait_recv()
            ur_.wait_recv()

    def sent(r_, d_, u_, dr_, ur_):
        r_.wait_send()

        @pl.when(has_down)
        def _():
            d_.wait_send()
            dr_.wait_send()

        @pl.when(has_up)
        def _():
            u_.wait_send()
            ur_.wait_send()

    moves = (go_right, go_down, go_up, go_down_right, go_up_right)
    exchange(*moves)

    a = shifts[0, 0]
    b = shifts[0, 1]

    sr, sl, sc = slot_parts(col(WIN))
    for jc in range(2):
        c = sc + (WLON * jc) - b
        target = jnp.where(c >= 0, (sr + REACH - a) * LINE + sl * COLS + c, -1)
        sel_own[jc] = onehot(target, row(SPAN))
    c = sc - b
    for jr in range(3):
        r = sr + (WLAT * jr) - a
        place = jnp.where(
            r < 0, 128 + (r + REACH) * 10, jnp.where(r < ROWS, r * 10, 192 + (r - ROWS) * 10)
        )
        target = jnp.where(c < 0, place + sl * 5 + c + REACH, -1)
        sel_side[jr] = onehot(target, row(256))

    q = col(TOK)
    half = div(q, HALF)
    k = div(q - half * HALF, HALF2)
    cr, clev, cc = own_parts(q - half * HALF - k * HALF2)
    fr = cr * 2 + (k & 1)
    fc = (cc + half * (COLS2 // 2)) * 2 + (k >> 1)
    resid[...] = mm(
        onehot(fr * LINE + clev * COLS + fc, row(TOK)), inputs[...].reshape(TOK, D1)
    )
    up = fr + a
    jr = div(up, WLAT)
    over = fc + b
    jc = div(over, WLON)
    slot = ((up - jr * WLAT) * 2 + clev) * WLON + (over - jc * WLON)
    lanes = row(256)
    lanes = jnp.where(lanes < MAIN, lanes, MAIN + (lanes & 15))
    for w in range(6):
        target = jnp.where((jr == w % 3) & (jc == w // 3), slot, -1)
        sel_back[:, w * 256 : (w + 1) * 256] = onehot(target, lanes)
    target = jnp.where(
        jc == 2, jr * 64 + ((up - jr * WLAT) * 2 + clev) * REACH + over - COLS, -1
    )
    sel_back[:, 6 * 256 :] = onehot(target, row(192))

    loads[0].wait()

    def key_bias(jr, rows, a, lat_rows):
        r = sr + jr * WLAT - a + lat * rows
        return jnp.where((r >= 0) & (r < lat_rows), 0.0, NEGATIVE).astype(F32)

    def project(at, x):
        qkv[at * WIN : (at + 1) * WIN] = mm(x, w_qkv[...]).astype(BF)

    def gather(jr, jc):
        x = mm(sel_own[jc], ext[WLAT * jr : WLAT * jr + WLAT + REACH].reshape(SPAN, D1))
        if jc == 0:
            n = 128 if jr == 1 else 256
            x = x + mm(sel_side[jr, :, 0:n], side[0:n])
        return x.astype(BF)

    def attend(at, jr, jc):
        base = at * WIN
        lane0 = (jc * 3 + jr) * 256

        def put(r0, rn, l0, ln, value):
            mixed[r0 : r0 + rn, lane0 + l0 : lane0 + l0 + ln] = value.astype(BF)

        window_attend(
            lambda rows, part: qkv[pl.ds(base + rows.start, rows.size), part],
            lambda part: qkv[pl.ds(base, WIN), pl.ds(D1 + part.start, part.size)],
            lambda part: qkv[pl.ds(base, WIN), pl.ds(2 * D1 + part.start, part.size)],
            D1,
            key_bias(jr, ROWS, a, ROWS * lat_n),
            put,
        )

    s = col(64)
    r = div(s, 10)
    rest = s - r * 10
    lev = div(rest, 5)
    first = jnp.where(r < WLAT, (r * 2 + lev) * WLON + rest - lev * 5, -1)
    pick_first = onehot(first, lanes)
    returns = []

    def give_back(jr):
        part = pl.ds(jr * 64, 64)
        back_out[part, :] = mm_nt(pick_first, mixed[:, jr * 256 : (jr + 1) * 256]).astype(BF)
        copy = remote(11 + jr, back_out.at[part], back_in.at[part], lat, left)
        copy.start()
        returns.append(copy)

    project(0, gather(1, 1))
    attend(0, 1, 1)
    moves[0].wait_recv()
    project(1, gather(1, 0))
    attend(1, 1, 0)
    give_back(1)

    arrived(*moves[1:])
    for at, jr in ((2, 0), (3, 2)):
        project(at, gather(jr, 0))
        attend(at, jr, 0)
        give_back(jr)

    project(4, gather(0, 1))
    project(5, gather(2, 1))
    attend(4, 0, 1)
    attend(5, 2, 1)

    loads[1].wait()
    loads[2].wait()
    loads[3].wait()
    loads[4].wait()
    a2 = shifts[1, 0]
    b2 = shifts[1, 1]

    def message(i, there, d_lat, d_lon):
        part = pl.ds(i * 64, 64)
        return remote(i + 14, send2.at[part], ext2.at[part], there + d_lat, d_lon)

    downs = [message(i, lat, 1, lon) for i in (0, 2)] + [message(5, lat, 1, right)]
    ups = [message(i, lat, -1, lon) for i in (1, 3)] + [message(6, lat, -1, right)]
    right2 = message(4, lat, 0, right)
    goes_up = even & has_up
    from_below = odd & has_down

    s = col(64)
    rl6 = div(s, 6)
    lines = rl6 * 6 + (s - rl6 * 6)
    rl5 = div(s, 5)
    columns = rl5 * 6 + (s - rl5 * 5) + 1
    top = jnp.where(s < 60, lines, -1)
    bottom = jnp.where(s < 60, lines + 12, -1)
    aside = jnp.where(s < 60, columns, -1)
    aside_bottom = jnp.where(s < 50, columns + 12, -1)
    aside_top = jnp.where(s < 50, columns, -1)

    coarse = []
    for h in range(2):
        if h == 1:
            for copy in returns:
                copy.wait_recv()
        part = slice(h * HALF, (h + 1) * HALF)
        own = mm_nt(sel_back[part, 0 : 6 * 256], mixed[...])
        if h == 1:
            own = own + mm(sel_back[part, 6 * 256 :], back_in[...])
        attended = (resid[part] + mm(own.astype(BF), w_out[...])).astype(BF)
        total = attended.astype(F32)
        x = norm(total, gain_mlp[...])
        acc[part] = total
        chunk = 512
        for i in range(FF1 // chunk):
            y = mm(x, w_up[:, i * chunk : (i + 1) * chunk])
            y = jax.nn.gelu(y).astype(BF)
            acc[part] += mm(y, w_down[i * chunk : (i + 1) * chunk, :])
        total = acc[part].astype(BF).astype(F32)
        acc[part] = total
        merged = jnp.concatenate(
            [total[k * HALF2 : (k + 1) * HALF2] for k in range(4)], axis=1
        )
        merged = mm(norm(merged, gain_merge[...]), w_merge[...]).astype(BF).astype(F32)
        coarse.append(merged)
        normed = norm(merged, gain_coarse[...])
        norm2[h] = normed.astype(F32)
        if h == 0:
            pick = jnp.concatenate([bottom, top], axis=0)
            send2[0:128] = mm(onehot(pick, row(HALF2)), normed).astype(BF)
        else:
            pick = jnp.concatenate([bottom, top, aside, aside_bottom, aside_top], axis=0)
            send2[128:448] = mm(onehot(pick, row(HALF2)), normed).astype(BF)
            right2.start()

        @pl.when(has_down)
        def _():
            for copy in downs[h : 2 * h + 1]:
                copy.start()

        @pl.when(goes_up)
        def _():
            for copy in ups[h : 2 * h + 1]:
                copy.start()


    c = sc - b2
    for w in range(2):
        r = sr + WLAT * w - a2
        inside = (r >= 0) & (r < ROWS2)
        right_half = jnp.where(c >= 6, 1, 0)
        place = (r * 2 + sl) * 6 + c - right_half * 6
        for h in range(2):
            target = jnp.where(inside & (c >= 0) & (right_half == h), place, -1)
            sel2_own[w, h] = onehot(target, row(HALF2))
        beyond = jnp.where(r < 0, r + REACH, r - ROWS2)
        beyond = jnp.where(beyond < REACH, beyond, -1000)
        line = jnp.where(r < 0, 0, 64) + right_half * 128 + (beyond * 2 + sl) * 6 + c - right_half * 6
        corner = jnp.where(r < 0, 320, 384) + (beyond * 2 + sl) * 5 + c + REACH
        aside = 256 + (r * 2 + sl) * 5 + c + REACH
        target = jnp.where(
            inside, jnp.where(c < 0, aside, -1), jnp.where(c < 0, corner, line)
        )
        sel2[w * WIN : (w + 1) * WIN, :] = onehot(target, row(448))

    def collect(w):
        x = mm(sel2[w * WIN : (w + 1) * WIN, :], ext2[...])
        for h in range(2):
            x = x + mm(sel2_own[w, h], norm2[h].astype(BF))
        return x.astype(BF)

    lanes = row(held)
    lanes = jnp.where(lanes < MAIN, lanes, MAIN + (lanes & 15))
    pick_here, pick_there = [], []
    for h in range(2):
        rr, ll, cc = own_parts(col(HALF2) + h * HALF2)
        up = rr + a2
        over = cc + b2
        here = (up < WLAT) & (over < COLS2)
        pick_here.append(onehot(jnp.where(here, (up * 2 + ll) * WLON + over, -1), lanes))
        below = up >= WLAT
        up = jnp.where(below, up - WLAT, up)
        target = jnp.where(
            over < COLS2,
            jnp.where(below, (up * 2 + ll) * WLON + over, -1),
            jnp.where(below, 192, 128) + (up * 2 + ll) * REACH + over - COLS2,
        )
        pick_there.append(onehot(target, row(256)))
    s = col(192)
    target = jnp.where(s < 128, s, jnp.concatenate([jnp.zeros((128, 1), I32), first], axis=0))
    pick_out = onehot(target, lanes)

    loads[5].wait()
    right2.wait_recv()

    @pl.when(has_up)
    def _():
        for copy in downs:
            copy.wait_recv()

    @pl.when(from_below)
    def _():
        for copy in ups:
            copy.wait_recv()

    x2[0:WIN] = collect(0)

    @pl.when(even)
    def _():
        for i in range(3):
            part = slice(i * D2, (i + 1) * D2)
            qkv2[0:WIN, part] = mm(x2[0:WIN], w_qkv2[:, part]).astype(BF)

    @pl.when(odd)
    def _():
        x2[WIN:] = collect(1)
        for i in range(3):
            part = slice(i * D2, (i + 1) * D2)
            qkv2[:, part] = mm(x2[...], w_qkv2[:, part]).astype(BF)

    def attend2(w):
        base = w * WIN

        def put(r0, rn, l0, ln, value):
            mixed2[r0 : r0 + rn, l0 : l0 + ln] = value.astype(BF)

        window_attend(
            lambda rows, part: qkv2[pl.ds(base + rows.start, rows.size), part],
            lambda part: qkv2[pl.ds(base, WIN), pl.ds(D2 + part.start, part.size)],
            lambda part: qkv2[pl.ds(base, WIN), pl.ds(2 * D2 + part.start, part.size)],
            D2,
            key_bias(w, ROWS2, a2, ROWS2 * lat_n),
            put,
        )

    attend2(0)
    back2_out[...] = mm_nt(pick_out, mixed2[...]).astype(BF)
    left2 = remote(5, back2_out.at[128:192], back2_in.at[128:192], lat, left)
    up2 = remote(6, back2_out.at[0:128], back2_in.at[0:128], lat - 1, lon)
    up_left2 = remote(7, back2_out.at[128:192], back2_in.at[192:256], lat - 1, left)
    last_left2 = remote(8, last_out, back2_in.at[192:256], lat, left)

    @pl.when(odd)
    def _():
        up2.start()
        up_left2.start()

    left2.start()
    own2 = [mm_nt(pick, mixed2[...]) for pick in pick_here]

    @pl.when(odd)
    def _():
        attend2(1)
        leaving = mm_nt(pick_out, mixed2[...]).astype(BF)
        back2_in[0:128] = leaving[0:128]
        last_out[...] = leaving[128:192]
        last_left2.start()

    loads[6].wait()
    loads[7].wait()

    @pl.when(even)
    def _():
        up2.wait_recv()

    for h in range(2):
        if h == 0:
            other = mm(pick_there[0][:, 0:128], back2_in[0:128])
        else:
            left2.wait_recv()

            @pl.when(even)
            def _():
                up_left2.wait_recv()

            @pl.when(odd)
            def _():
                last_left2.wait_recv()

            other = mm(pick_there[1], back2_in[...])
        coarse_out = (coarse[h] + mm((own2[h] + other).astype(BF), w_out2[...])).astype(BF)
        for k in range(4):
            at = h * HALF + k * HALF2
            spread = mm(coarse_out, w_expand[:, k * D1 : (k + 1) * D1])
            acc[at : at + HALF2] = acc[at : at + HALF2] + spread

    t = col(TOK)
    lev = div(t, ROWS * COLS)
    rest = t - lev * (ROWS * COLS)
    r = div(rest, COLS)
    c = rest - r * COLS
    half = jnp.where(c >= COLS // 2, 1, 0)
    quadrant = (c & 1) * 2 + (r & 1)
    target = half * HALF + quadrant * HALF2 + ((r >> 1) * 2 + lev) * 6 + (c >> 1) - half * 6
    final = mm(onehot(target, row(TOK)), acc[...].astype(BF))
    out[...] = final.reshape(2, ROWS, COLS, D1).astype(BF)

    sent(*moves)
    right2.wait_send()
    left2.wait_send()

    @pl.when(has_down)
    def _():
        for copy in downs:
            copy.wait_send()

    @pl.when(goes_up)
    def _():
        for copy in ups:
            copy.wait_send()

    @pl.when(odd)
    def _():
        up2.wait_send()
        up_left2.wait_send()
        last_left2.wait_send()

    for copy in returns:
        copy.wait_send()


def local(
    tokens, land_mask, land_embed, shifts, gain_attn, w_qkv_fine, w_out_fine, gain_mlp, w_up_fine,
    w_down_fine, gain_merge, w_merge, gain_coarse, w_qkv_coarse, w_out_coarse, w_expand,
):
    vmem = pl.BlockSpec(memory_space=pltpu.VMEM)
    hbm = pl.BlockSpec(memory_space=pl.ANY)
    smem = pl.BlockSpec(memory_space=pltpu.SMEM)
    weights = [
        w_qkv_fine, w_out_fine, w_up_fine, w_down_fine, w_merge, w_qkv_coarse, w_out_coarse, w_expand,
    ]
    V = pltpu.VMEM
    return pl.pallas_call(
        kernel,
        out_shape=jax.ShapeDtypeStruct(tokens.shape, BF),
        in_specs=[vmem, vmem, vmem, smem, vmem, vmem, vmem, vmem] + [hbm] * 8,
        out_specs=vmem,
        scratch_shapes=[V(w.shape, BF) for w in weights]
        + [
            V((ROWS, LINE, D1), BF),
            V((ROWS + 2 * REACH + 1, LINE, D1), BF),
            V((256, D1), BF),
            V((256, D1), BF),
            V((2, WIN, SPAN), BF),
            V((3, WIN, 256), BF),
            V((TOK, 6 * 256 + 192), BF),
            V((6 * WIN, 3 * D1), BF),
            V((D1, 6 * 256), BF),
            V((192, D1), BF),
            V((192, D1), BF),
            V((TOK, D1), F32),
            V((TOK, D1), F32),
            V((2, HALF2, D2), F32),
            V((448, D2), BF),
            V((448, D2), BF),
            V((2 * WIN, 448), BF),
            V((2, 2, WIN, HALF2), BF),
            V((2 * WIN, D2), BF),
            V((2 * WIN, 3 * D2), BF),
            V((D2, held), BF),
            V((192, D2), BF),
            V((64, D2), BF),
            V((256, D2), BF),
            pltpu.SemaphoreType.DMA((8,)),
            pltpu.SemaphoreType.DMA((21,)),
            pltpu.SemaphoreType.DMA((21,)),
        ],
        compiler_params=pltpu.CompilerParams(
            collective_id=0, has_side_effects=True, vmem_limit_bytes=56 * 1024 * 1024
        ),
    )(
        tokens, land_mask, land_embed.reshape(1, D1), shifts, gain_attn.reshape(1, D1),
        gain_mlp.reshape(1, D1), gain_merge.reshape(1, 4 * D1), gain_coarse.reshape(1, D2), *weights,
    )


def solution(mesh):
    spec = P(None, "lat", "lon", None)
    return jax.shard_map(
        local,
        mesh=mesh,
        in_specs=(spec, P("lat", "lon")) + (P(),) * 14,
        out_specs=spec,
        check_vma=False,
    )
```

profile of v0, /device:TPU:1, one launch (start us, length us, event | category | flops | bytes accessed | tf_op | source)
XLA Modules:
  0.0 56.6 jit_solution(10816042476124142106)
XLA Ops:
  0.0 54.7 %shard_map.154 = bf16[2,12,24,512]{3,2,1,0:T(8,128)(2,1)} custom-call(bf16[2,12,24,512]{3,2,1,0:T(8,128)(2,1)} %tokens.1, s32[12,24]{1,0:T(8,128)} %mask.1, f32[1,512]{1,0:T(1,128)} %bitcast.7, s32[2,2]{1,0:T(2,128)} %shifts.1, f32[1,512]{1,0:T(1,128)} %bitcast.8, f32[1,512]{1,0:T(1,128)} %bitcast.9, f32[1,2048]{1,0:T(1,128)} %bitcast.5, f32[1,1024]{1,0:T(1,128)} %bitcast.6, ...), custom_call_target="tpu_custom_call" | custom-call | tf_op jit(solution)/shard_map/pallas_call | solution.py:640
  54.7 1.9 %copy.18 = bf16[2,12,24,512]{3,2,1,0:T(8,128)(2,1)} copy(bf16[2,12,24,512]{3,2,1,0:T(8,128)(2,1)} %shard_map.154) | data formatting | bytes 1179648
where the time goes:
time: 57.1 us; the launch traced here: 56.6 us
  Pallas kernels  54.7 us (96%)
  local copies, waits for them, and re-layouts  1.92 us (3%)
    pallas_call x1, Pallas kernels, local(): pl.pallas_call(kernel, out_shape=jax.ShapeDtypeStruct(tokens.shape, BF),...  54.7 us
    unnamed x1, local copies, waits for them, and re-layouts  1.92 us

commit v1 on v0

--- a/solution.py
+++ b/solution.py
@@ -121,9 +121,10 @@
 
 
 def kernel(
-    tokens, mask, embed, shifts, gain_attn, gain_mlp, gain_merge, gain_coarse,
+    tokens_h, mask_h, embed_h, shifts, gain_attn_h, gain_mlp_h, gain_merge_h, gain_coarse_h,
     w_qkv_h, w_out_h, w_up_h, w_down_h, w_merge_h, w_qkv2_h, w_out2_h, w_expand_h,
     out,
+    tokens, mask, embed, gain_attn, gain_mlp, gain_merge, gain_coarse,
     w_qkv, w_out, w_up, w_down, w_merge, w_qkv2, w_out2, w_expand,
     inputs, ext, side_out, side, sel_own, sel_side, sel_back, qkv, mixed, back_out, back_in,
     resid, acc,
@@ -141,10 +142,30 @@
     odd = lax.rem(lat, 2) == 1
     even = jnp.logical_not(odd)
 
+    barrier = pltpu.get_barrier_semaphore()
+
+    def greet(a, b):
+        pl.semaphore_signal(barrier, inc=1, device_id=(a, b), device_id_type=MESH)
+
+    greet(lat, left)
+    greet(lat, right)
+
+    @pl.when(has_up)
+    def _():
+        for b in (left, lon, right):
+            greet(lat - 1, b)
+
+    @pl.when(has_down)
+    def _():
+        for b in (left, lon, right):
+            greet(lat + 1, b)
+
     loads = []
     for i, (src, dst) in enumerate(
         [
-            (w_qkv_h, w_qkv), (w_out_h, w_out), (w_up_h, w_up), (w_down_h, w_down),
+            (tokens_h, tokens), (mask_h, mask), (embed_h, embed), (gain_attn_h, gain_attn),
+            (w_qkv_h, w_qkv), (gain_mlp_h, gain_mlp), (gain_merge_h, gain_merge),
+            (gain_coarse_h, gain_coarse), (w_out_h, w_out), (w_up_h, w_up), (w_down_h, w_down),
             (w_merge_h, w_merge), (w_qkv2_h, w_qkv2), (w_out2_h, w_out2), (w_expand_h, w_expand),
         ]
     ):
@@ -152,30 +173,14 @@
         load.start()
         loads.append(load)
 
-    barrier = pltpu.get_barrier_semaphore()
-
-    def greet(a, b):
-        pl.semaphore_signal(barrier, inc=1, device_id=(a, b), device_id_type=MESH)
-
-    greet(lat, left)
-    greet(lat, right)
-
-    @pl.when(has_up)
-    def _():
-        for b in (left, lon, right):
-            greet(lat - 1, b)
-
-    @pl.when(has_down)
-    def _():
-        for b in (left, lon, right):
-            greet(lat + 1, b)
-
     def remote(i, src, dst, a, b):
         return pltpu.make_async_remote_copy(
             src_ref=src, dst_ref=dst, send_sem=send_sem.at[i], recv_sem=recv_sem.at[i],
             device_id=(a, b), device_id_type=MESH,
         )
 
+    for load in loads[:4]:
+        load.wait()
     eye = col(COLS) == row(COLS)
     add = embed[...]
     gain = gain_attn[...]
@@ -312,7 +317,7 @@
     )
     sel_back[:, 6 * 256 :] = onehot(target, row(192))
 
-    loads[0].wait()
+    loads[4].wait()
 
     def key_bias(jr, rows, a, lat_rows):
         r = sr + jr * WLAT - a + lat * rows
@@ -377,10 +382,8 @@
     attend(4, 0, 1)
     attend(5, 2, 1)
 
-    loads[1].wait()
-    loads[2].wait()
-    loads[3].wait()
-    loads[4].wait()
+    for load in loads[5:12]:
+        load.wait()
     a2 = shifts[1, 0]
     b2 = shifts[1, 1]
 
@@ -417,13 +420,8 @@
         attended = (resid[part] + mm(own.astype(BF), w_out[...])).astype(BF)
         total = attended.astype(F32)
         x = norm(total, gain_mlp[...])
-        acc[part] = total
-        chunk = 512
-        for i in range(FF1 // chunk):
-            y = mm(x, w_up[:, i * chunk : (i + 1) * chunk])
-            y = jax.nn.gelu(y).astype(BF)
-            acc[part] += mm(y, w_down[i * chunk : (i + 1) * chunk, :])
-        total = acc[part].astype(BF).astype(F32)
+        y = jax.nn.gelu(mm(x, w_up[...])).astype(BF)
+        total = (total + mm(y, w_down[...])).astype(BF).astype(F32)
         acc[part] = total
         merged = jnp.concatenate(
             [total[k * HALF2 : (k + 1) * HALF2] for k in range(4)], axis=1
@@ -497,7 +495,7 @@
     target = jnp.where(s < 128, s, jnp.concatenate([jnp.zeros((128, 1), I32), first], axis=0))
     pick_out = onehot(target, lanes)
 
-    loads[5].wait()
+    loads[12].wait()
     right2.wait_recv()
 
     @pl.when(has_up)
@@ -563,8 +561,8 @@
         last_out[...] = leaving[128:192]
         last_left2.start()
 
-    loads[6].wait()
-    loads[7].wait()
+    loads[13].wait()
+    loads[14].wait()
 
     @pl.when(even)
     def _():
@@ -639,10 +637,14 @@
     V = pltpu.VMEM
     return pl.pallas_call(
         kernel,
-        out_shape=jax.ShapeDtypeStruct(tokens.shape, BF),
-        in_specs=[vmem, vmem, vmem, smem, vmem, vmem, vmem, vmem] + [hbm] * 8,
+        out_shape=pltpu.VMEM(tokens.shape, BF),
+        in_specs=[hbm, hbm, hbm, smem] + [hbm] * 12,
         out_specs=vmem,
-        scratch_shapes=[V(w.shape, BF) for w in weights]
+        scratch_shapes=[
+            V(tokens.shape, BF), V(land_mask.shape, I32), V((1, D1), F32), V((1, D1), F32),
+            V((1, D1), F32), V((1, 4 * D1), F32), V((1, D2), F32),
+        ]
+        + [V(w.shape, BF) for w in weights]
         + [
             V((ROWS, LINE, D1), BF),
             V((ROWS + 2 * REACH + 1, LINE, D1), BF),
@@ -668,7 +670,7 @@
             V((192, D2), BF),
             V((64, D2), BF),
             V((256, D2), BF),
-            pltpu.SemaphoreType.DMA((8,)),
+            pltpu.SemaphoreType.DMA((15,)),
             pltpu.SemaphoreType.DMA((21,)),
             pltpu.SemaphoreType.DMA((21,)),
         ],

time: 57.1 us -> 53.7 us (0.940)
  Pallas kernels: 54.7 us -> 52.5 us
  local copies, waits for them, and re-layouts: 1.92 us -> 0.82 us
    pallas_call x1, Pallas kernels: 54.7 us -> 52.5 us  [local(): pl.pallas_call(kernel, out_shape=pltpu.VMEM(tokens.shape, BF), in_specs=[...]
    unnamed x1, local copies, waits for them, and re-layouts: 1.92 us -> 0.82 us
where the time goes in v1:
time: 53.7 us; the launch traced here: 53.3 us
  Pallas kernels  52.5 us (98%)
  local copies, waits for them, and re-layouts  0.82 us (2%)
    pallas_call x1, Pallas kernels, local(): pl.pallas_call(kernel, out_shape=pltpu.VMEM(tokens.shape, BF), in_specs=[...  52.5 us

profile of v1, /device:TPU:1, one launch (start us, length us, event | category | flops | bytes accessed | tf_op | source)
XLA Modules:
  0.0 53.3 jit_solution(593675524791959607)
XLA Ops:
  0.0 52.5 %shard_map.154 = bf16[2,12,24,512]{3,2,1,0:T(8,128)(2,1)S(1)} custom-call(bf16[2,12,24,512]{3,2,1,0:T(8,128)(2,1)} %tokens_h.1, s32[12,24]{1,0:T(8,128)} %mask_h.1, f32[1,512]{1,0:T(1,128)} %bitcast.7, s32[2,2]{1,0:T(2,128)} %shifts.1, f32[1,512]{1,0:T(1,128)} %bitcast.8, f32[1,512]{1,0:T(1,128)} %bitcast.9, f32[1,2048]{1,0:T(1,128)} %bitcast.5, ...), custom_call_target="tpu_custom_call" | custom-call | tf_op jit(solution)/shard_map/pallas_call | solution.py:638
  52.5 0.8 %copy.18 = bf16[2,12,24,512]{3,2,1,0:T(8,128)(2,1)} copy(bf16[2,12,24,512]{3,2,1,0:T(8,128)(2,1)S(1)} %shard_map.154) | data formatting | bytes 1179648

commit v2 on v1

--- a/solution.py
+++ b/solution.py
@@ -16,7 +16,7 @@
 D1 = 512
 D2 = 1024
 FF1 = 2048
-held = MAIN + REST * (D2 // HEAD)
+held = MAIN + REST * (D1 // HEAD)
 ROWS, COLS = 12, 24
 ROWS2, COLS2 = 6, 12
 TOK = 2 * ROWS * COLS
@@ -128,7 +128,7 @@
     w_qkv, w_out, w_up, w_down, w_merge, w_qkv2, w_out2, w_expand,
     inputs, ext, side_out, side, sel_own, sel_side, sel_back, qkv, mixed, back_out, back_in,
     resid, acc,
-    norm2, send2, ext2, sel2, sel2_own, x2, qkv2, mixed2, back2_out, last_out, back2_in,
+    norm2, send2, ext2, sel2, sel2_own, x2, qkv2, mixed2, back2_out, last_out, back2_in, sel_out,
     w_sem, send_sem, recv_sem,
 ):
     lat = lax.axis_index("lat")
@@ -184,13 +184,19 @@
     eye = col(COLS) == row(COLS)
     add = embed[...]
     gain = gain_attn[...]
-    for r in range(ROWS):
-        land = jnp.sum(jnp.where(eye, mask[r : r + 1, :].astype(F32), 0.0), axis=1, keepdims=True)
-        x = jnp.concatenate(
-            [tokens[0, r].astype(F32) + land * add, tokens[1, r].astype(F32) + land * add], axis=0
-        ).astype(BF)
-        inputs[r] = x
-        ext[REACH + r] = norm(x.astype(F32), gain)
+    lands = [
+        jnp.sum(jnp.where(eye, mask[r : r + 1, :].astype(F32), 0.0), axis=1, keepdims=True)
+        for r in range(ROWS)
+    ]
+    for group in range(0, ROWS, 4):
+        lines = []
+        for r in range(group, group + 4):
+            shift = lands[r] * add
+            lines += [tokens[0, r].astype(F32) + shift, tokens[1, r].astype(F32) + shift]
+        x = jnp.concatenate(lines, axis=0).astype(BF)
+        inputs[group : group + 4] = x.reshape(4, LINE, D1)
+        x = norm(x.astype(F32), gain)
+        ext[REACH + group : REACH + group + 4] = x.reshape(4, LINE, D1)
 
     s = col(256)
     part = jnp.where(s < 128, 0, jnp.where(s < 192, 1, 2))
@@ -323,8 +329,9 @@
         r = sr + jr * WLAT - a + lat * rows
         return jnp.where((r >= 0) & (r < lat_rows), 0.0, NEGATIVE).astype(F32)
 
-    def project(at, x):
-        qkv[at * WIN : (at + 1) * WIN] = mm(x, w_qkv[...]).astype(BF)
+    def project(at, *xs):
+        x = jnp.concatenate(xs, axis=0)
+        qkv[at * WIN : (at + len(xs)) * WIN] = mm(x, w_qkv[...]).astype(BF)
 
     def gather(jr, jc):
         x = mm(sel_own[jc], ext[WLAT * jr : WLAT * jr + WLAT + REACH].reshape(SPAN, D1))
@@ -372,13 +379,12 @@
     give_back(1)
 
     arrived(*moves[1:])
+    project(2, gather(0, 0), gather(2, 0))
     for at, jr in ((2, 0), (3, 2)):
-        project(at, gather(jr, 0))
         attend(at, jr, 0)
         give_back(jr)
 
-    project(4, gather(0, 1))
-    project(5, gather(2, 1))
+    project(4, gather(0, 1), gather(2, 1))
     attend(4, 0, 1)
     attend(5, 2, 1)
 
@@ -523,86 +529,111 @@
             part = slice(i * D2, (i + 1) * D2)
             qkv2[:, part] = mm(x2[...], w_qkv2[:, part]).astype(BF)
 
-    def attend2(w):
+    def attend2(w, g):
         base = w * WIN
 
         def put(r0, rn, l0, ln, value):
-            mixed2[r0 : r0 + rn, l0 : l0 + ln] = value.astype(BF)
+            mixed2[g * D1 + r0 : g * D1 + r0 + rn, l0 : l0 + ln] = value.astype(BF)
+
+        def at(block, part):
+            return pl.ds(block * D2 + g * D1 + part.start, part.size)
 
         window_attend(
-            lambda rows, part: qkv2[pl.ds(base + rows.start, rows.size), part],
-            lambda part: qkv2[pl.ds(base, WIN), pl.ds(D2 + part.start, part.size)],
-            lambda part: qkv2[pl.ds(base, WIN), pl.ds(2 * D2 + part.start, part.size)],
-            D2,
+            lambda rows, part: qkv2[pl.ds(base + rows.start, rows.size), at(0, part)],
+            lambda part: qkv2[pl.ds(base, WIN), at(1, part)],
+            lambda part: qkv2[pl.ds(base, WIN), at(2, part)],
+            D1,
             key_bias(w, ROWS2, a2, ROWS2 * lat_n),
             put,
         )
-
-    attend2(0)
-    back2_out[...] = mm_nt(pick_out, mixed2[...]).astype(BF)
-    left2 = remote(5, back2_out.at[128:192], back2_in.at[128:192], lat, left)
-    up2 = remote(6, back2_out.at[0:128], back2_in.at[0:128], lat - 1, lon)
-    up_left2 = remote(7, back2_out.at[128:192], back2_in.at[192:256], lat - 1, left)
-    last_left2 = remote(8, last_out, back2_in.at[192:256], lat, left)
+        return mm_nt(pick_out, mixed2[g * D1 : (g + 1) * D1, :]).astype(BF)
+
+    left2, up2, up_left2, last_left2 = [], [], [], []
+    for g in range(2):
+        back2_out[g] = attend2(0, g)
+        column = back2_out.at[g, 128:192]
+        left2.append(remote(5 + g, column, back2_in.at[g, 128:192], lat, left))
+        up2.append(remote(7 + g, back2_out.at[g, 0:128], back2_in.at[g, 0:128], lat - 1, lon))
+        up_left2.append(remote(9 + g, column, back2_in.at[g, 192:256], lat - 1, left))
+        last_left2.append(remote(21 + g, last_out.at[g], back2_in.at[g, 192:256], lat, left))
+
+        @pl.when(odd)
+        def _():
+            up2[g].start()
+            up_left2[g].start()
+
+        left2[g].start()
+
+    own2 = [mm_nt(pick, mixed2[...]) for pick in pick_here]
 
     @pl.when(odd)
     def _():
-        up2.start()
-        up_left2.start()
-
-    left2.start()
-    own2 = [mm_nt(pick, mixed2[...]) for pick in pick_here]
-
-    @pl.when(odd)
-    def _():
-        attend2(1)
-        leaving = mm_nt(pick_out, mixed2[...]).astype(BF)
-        back2_in[0:128] = leaving[0:128]
-        last_out[...] = leaving[128:192]
-        last_left2.start()
-
-    loads[13].wait()
-    loads[14].wait()
-
-    @pl.when(even)
-    def _():
-        up2.wait_recv()
-
-    for h in range(2):
-        if h == 0:
-            other = mm(pick_there[0][:, 0:128], back2_in[0:128])
-        else:
-            left2.wait_recv()
-
-            @pl.when(even)
-            def _():
-                up_left2.wait_recv()
-
-            @pl.when(odd)
-            def _():
-                last_left2.wait_recv()
-
-            other = mm(pick_there[1], back2_in[...])
-        coarse_out = (coarse[h] + mm((own2[h] + other).astype(BF), w_out2[...])).astype(BF)
-        for k in range(4):
-            at = h * HALF + k * HALF2
-            spread = mm(coarse_out, w_expand[:, k * D1 : (k + 1) * D1])
-            acc[at : at + HALF2] = acc[at : at + HALF2] + spread
+        for g in range(2):
+            leaving = attend2(1, g)
+            back2_in[g, 0:128] = leaving[0:128]
+            last_out[g] = leaving[128:192]
+            last_left2[g].start()
 
     t = col(TOK)
     lev = div(t, ROWS * COLS)
     rest = t - lev * (ROWS * COLS)
     r = div(rest, COLS)
     c = rest - r * COLS
-    half = jnp.where(c >= COLS // 2, 1, 0)
+    side_of = jnp.where(c >= COLS // 2, 1, 0)
     quadrant = (c & 1) * 2 + (r & 1)
-    target = half * HALF + quadrant * HALF2 + ((r >> 1) * 2 + lev) * 6 + (c >> 1) - half * 6
-    final = mm(onehot(target, row(TOK)), acc[...].astype(BF))
+    target = quadrant * HALF2 + ((r >> 1) * 2 + lev) * 6 + (c >> 1) - side_of * 6
+    for h in range(2):
+        sel_out[h] = onehot(jnp.where(side_of == h, target, -1), row(HALF))
+
+    loads[13].wait()
+    loads[14].wait()
+
+    @pl.when(even)
+    def _():
+        for copy in up2:
+            copy.wait_recv()
+
+    def returned(h, rows):
+        pick = pick_there[h][:, 0:rows]
+        return jnp.concatenate([mm(pick, back2_in[g, 0:rows]) for g in range(2)], axis=1)
+
+    final = None
+    for h in range(2):
+        if h == 0:
+            other = returned(0, 128)
+        else:
+            for g in range(2):
+                left2[g].wait_recv()
+
+            @pl.when(even)
+            def _():
+                for copy in up_left2:
+                    copy.wait_recv()
+
+            @pl.when(odd)
+            def _():
+                for copy in last_left2:
+                    copy.wait_recv()
+
+            other = returned(1, 256)
+        coarse_out = (coarse[h] + mm((own2[h] + other).astype(BF), w_out2[...])).astype(BF)
+        spread = mm(coarse_out, w_expand[...])
+        blended = jnp.concatenate(
+            [
+                acc[h * HALF + k * HALF2 : h * HALF + (k + 1) * HALF2]
+                + spread[:, k * D1 : (k + 1) * D1]
+                for k in range(4)
+            ],
+            axis=0,
+        )
+        placed = mm(sel_out[h], blended.astype(BF))
+        final = placed if h == 0 else final + placed
     out[...] = final.reshape(2, ROWS, COLS, D1).astype(BF)
 
     sent(*moves)
     right2.wait_send()
-    left2.wait_send()
+    for copy in left2:
+        copy.wait_send()
 
     @pl.when(has_down)
     def _():
@@ -616,9 +647,8 @@
 
     @pl.when(odd)
     def _():
-        up2.wait_send()
-        up_left2.wait_send()
-        last_left2.wait_send()
+        for copy in up2 + up_left2 + last_left2:
+            copy.wait_send()
 
     for copy in returns:
         copy.wait_send()
@@ -667,12 +697,13 @@
             V((2 * WIN, D2), BF),
             V((2 * WIN, 3 * D2), BF),
             V((D2, held), BF),
-            V((192, D2), BF),
-            V((64, D2), BF),
-            V((256, D2), BF),
+            V((2, 192, D1), BF),
+            V((2, 64, D1), BF),
+            V((2, 256, D1), BF),
+            V((2, TOK, HALF), BF),
             pltpu.SemaphoreType.DMA((15,)),
-            pltpu.SemaphoreType.DMA((21,)),
-            pltpu.SemaphoreType.DMA((21,)),
+            pltpu.SemaphoreType.DMA((23,)),
+            pltpu.SemaphoreType.DMA((23,)),
         ],
         compiler_params=pltpu.CompilerParams(
             collective_id=0, has_side_effects=True, vmem_limit_bytes=56 * 1024 * 1024

time: 53.7 us -> 53.4 us (level)
  no operation moved by 1% of the time
where the time goes in v2:
time: 53.4 us; the launch traced here: 53.2 us
  Pallas kernels  52.4 us (98%)
  local copies, waits for them, and re-layouts  0.82 us (2%)
    pallas_call x1, Pallas kernels, local(): pl.pallas_call(kernel, out_shape=pltpu.VMEM(tokens.shape, BF), in_specs=[...  52.4 us

profile of v2, /device:TPU:1, one launch (start us, length us, event | category | flops | bytes accessed | tf_op | source)
XLA Modules:
  0.0 53.2 jit_solution(17711501753097155348)
XLA Ops:
  0.0 52.4 %shard_map.154 = bf16[2,12,24,512]{3,2,1,0:T(8,128)(2,1)S(1)} custom-call(bf16[2,12,24,512]{3,2,1,0:T(8,128)(2,1)} %tokens_h.1, s32[12,24]{1,0:T(8,128)} %mask_h.1, f32[1,512]{1,0:T(1,128)} %bitcast.7, s32[2,2]{1,0:T(2,128)} %shifts.1, f32[1,512]{1,0:T(1,128)} %bitcast.8, f32[1,512]{1,0:T(1,128)} %bitcast.9, f32[1,2048]{1,0:T(1,128)} %bitcast.5, ...), custom_call_target="tpu_custom_call" | custom-call | tf_op jit(solution)/shard_map/pallas_call | solution.py:668
  52.4 0.8 %copy.18 = bf16[2,12,24,512]{3,2,1,0:T(8,128)(2,1)} copy(bf16[2,12,24,512]{3,2,1,0:T(8,128)(2,1)S(1)} %shard_map.154) | data formatting | bytes 1179648
